TPU v7x, 256 devices: a whole 4x4x8 slice. The times are simulated.
256 devices in a mesh: frames: 8 (over z_lo, x), dp: 32 (over y, z_hi, core).
Axes of the slice: x: 4, y: 4, z: 8 (z_hi: 4, z_lo: 2; z = z_hi * 2 + z_lo), core: 2. Of those that a mesh axis runs over, the one named last changes fastest.
Arguments:
- latents: bfloat16 [32, 16, 144, 640], P('dp', 'frames'), may hold values from -80 to 80
- pose: int32 [32, 16, 144], P('dp', 'frames'), may hold values from 0 to 18
- timesteps: int32 [32], P('dp'), may hold values from 0 to 999
- norm_gain: float32 [640], replicated, may hold values from 0.1 to 1.9
- norm_bias: float32 [640], replicated, may hold values from -0.5 to 0.5
- pose_table: float32 [19, 640], replicated, may hold values from -6 to 6
- time_weight: float32 [320, 640], replicated, may hold values from -0.3125 to 0.3125
- spatial_weight: bfloat16 [5760, 640], P('dp'), may hold values from -0.078125 to 0.078125
- temporal_weight: bfloat16 [1920, 640], P('dp'), may hold values from -0.125 to 0.125
- cotangent: bfloat16 [32, 16, 144, 640], P('dp', 'frames'), may hold values from -16 to 16
Outputs:
- mixed: float32 [32, 16, 144, 640], P('dp', 'frames')
- latent_grad: float32 [32, 16, 144, 640], P('dp', 'frames')
- temporal_grad: float32 [1920, 640], P('dp')
All inputs are finite; a program needn't handle non-finite values.
Results may differ from a plain program's by a relative error of at most 0.0053.
Values may be sent and summed in bfloat16 or wider, within the bound.
No kernel may reach another device: no remote copies, remote signals or barrier semaphores. Data moves between devices by JAX's collectives and lax.ppermute only.
A program may use at most 128 MiB of HBM per device.

v0:
```python
import math
import jax
import jax.numpy as jnp
from jax import lax
from jax.sharding import PartitionSpec as P

GROUP_CH = 40
HT = 9
WD = 16


def silu_slope(value):
    gate = jax.nn.sigmoid(value)
    return gate * (1.0 + value * (1.0 - gate))


def spatial_cols(field, sign):
    count_n, height, width, chans = field.shape
    padded = jnp.pad(field, ((0, 0), (1, 1), (1, 1), (0, 0)))
    pieces = []
    for row_tap in range(3):
        for col_tap in range(3):
            top = 1 + sign * (row_tap - 1)
            left = 1 + sign * (col_tap - 1)
            pieces.append(padded[:, top : top + height, left : left + width, :])
    return jnp.concatenate(pieces, axis=-1).reshape(count_n * height * width, 9 * chans)


def temporal_cols(extended, frame_span, sign):
    pieces = []
    for tap in range(3):
        begin = 1 + sign * (tap - 1)
        pieces.append(extended[:, begin : begin + frame_span])
    joined = jnp.concatenate(pieces, axis=-1)
    return joined.reshape(-1, joined.shape[-1])


def time_shift(timesteps, time_weight):
    half = time_weight.shape[0] // 2
    positions = jnp.arange(half, dtype=jnp.float32)
    frequencies = jnp.exp(-math.log(10000.0) * positions / half)
    angles = timesteps.astype(jnp.float32)[:, None] * frequencies[None, :]
    embedding = jnp.concatenate([jnp.cos(angles), jnp.sin(angles)], axis=-1)
    return jnp.dot(embedding, time_weight, precision=lax.Precision.HIGHEST)


def pose_rows(pose, pose_table):
    kinds = jnp.arange(pose_table.shape[0], dtype=jnp.int32)
    onehot = (pose[..., None] == kinds).astype(jnp.float32)
    return jnp.dot(onehot, pose_table, precision=lax.Precision.HIGHEST)


def pad_frames(field):
    return jnp.pad(field, ((0, 0), (1, 1), (0, 0), (0, 0)))


def per_device(
    latents,
    pose,
    timesteps,
    norm_gain,
    norm_bias,
    pose_table,
    time_weight,
    spatial_weight,
    temporal_weight,
    cotangent,
):
    clips_dev, frames_dev, pixels, chans = latents.shape
    groups = chans // GROUP_CH
    frames_all = frames_dev * lax.axis_size("frames")
    clips_all = clips_dev * lax.axis_size("dp")
    entries = float(pixels * GROUP_CH)
    row_count = clips_dev * frames_dev * pixels
    factor = 1.0 / math.sqrt(clips_all * frames_all * pixels)
    shifted = latents.astype(jnp.float32) + pose_rows(pose, pose_table)
    grouped = shifted.reshape(clips_dev, frames_dev, pixels, groups, GROUP_CH)
    center = jnp.sum(grouped, axis=(2, 4)) / entries
    variance = jnp.sum(grouped * grouped, axis=(2, 4)) / entries - center * center
    inv_std = lax.rsqrt(variance + 1e-05)[:, :, None, :, None]
    normed_g = (grouped - center[:, :, None, :, None]) * inv_std
    normed = normed_g.reshape(clips_dev, frames_dev, pixels, chans)
    before = normed * norm_gain + norm_bias
    activated = jax.nn.silu(before).astype(jnp.bfloat16)
    act_cols = spatial_cols(activated.reshape(clips_dev * frames_dev, HT, WD, chans), 1)
    columns = act_cols
    convolved = jnp.dot(
        columns,
        lax.all_gather(spatial_weight, "dp", axis=0, tiled=True),
        preferred_element_type=jnp.float32,
    )
    shifts = time_shift(timesteps, time_weight)
    spatial_out = (
        convolved.reshape(clips_dev, frames_dev, pixels, chans) + shifts[:, None, None, :]
    ).astype(jnp.bfloat16)
    local_out = lax.all_to_all(spatial_out, "frames", split_axis=2, concat_axis=1, tiled=True)
    extended = pad_frames(local_out)
    moved_ext = jax.nn.silu(extended.astype(jnp.float32)).astype(jnp.bfloat16)
    moved_cols = temporal_cols(moved_ext, frames_all, 1)
    columns = moved_cols
    temporal_out = jnp.dot(
        columns,
        lax.all_gather(temporal_weight, "dp", axis=0, tiled=True),
        preferred_element_type=jnp.float32,
    )
    local_mixed = local_out.astype(jnp.float32) + temporal_out.reshape(local_out.shape)
    mixed = lax.all_to_all(local_mixed, "frames", split_axis=1, concat_axis=2, tiled=True)
    grad_local = lax.all_to_all(cotangent, "frames", split_axis=2, concat_axis=1, tiled=True)
    grad_ext = pad_frames(grad_local)
    grad_cols = temporal_cols(grad_ext, frames_all, -1)
    temporal_back = lax.all_gather(temporal_weight, "dp", axis=0, tiled=True)
    back_moved = jnp.einsum(
        "rtc,tkc->rk",
        grad_cols.reshape(row_count, 3, chans),
        temporal_back.reshape(3, chans, chans),
        preferred_element_type=jnp.float32,
    )
    back_local = (
        grad_local.astype(jnp.float32)
        + back_moved.reshape(grad_local.shape) * silu_slope(local_out.astype(jnp.float32))
    ).astype(jnp.bfloat16)
    grad_flat = grad_local.reshape(row_count, chans)
    columns = moved_cols
    owned = lax.psum_scatter(
        lax.dot_general(
            columns, grad_flat, (((0,), (0,)), ((), ())), preferred_element_type=jnp.float32
        ),
        "dp",
        scatter_dimension=0,
        tiled=True,
    )
    temporal_grad = lax.psum(owned, "frames") * factor
    back_spatial = lax.all_to_all(back_local, "frames", split_axis=1, concat_axis=2, tiled=True)
    spatial_back = lax.all_gather(spatial_weight, "dp", axis=0, tiled=True)
    back_cols = spatial_cols(back_spatial.reshape(clips_dev * frames_dev, HT, WD, chans), -1)
    back_act = jnp.einsum(
        "rtc,tkc->rk",
        back_cols.reshape(row_count, 9, chans),
        spatial_back.reshape(9, chans, chans),
        preferred_element_type=jnp.float32,
    )
    back_normed = (
        back_act.reshape(clips_dev, frames_dev, pixels, chans) * silu_slope(before) * norm_gain
    )
    back_grouped = back_normed.reshape(clips_dev, frames_dev, pixels, groups, GROUP_CH)
    first_mean = (jnp.sum(back_grouped, axis=(2, 4)) / entries)[:, :, None, :, None]
    second_mean = (jnp.sum(back_grouped * normed_g, axis=(2, 4)) / entries)[:, :, None, :, None]
    latent_grad = inv_std * (back_grouped - first_mean - normed_g * second_mean)
    latent_grad = latent_grad.reshape(clips_dev, frames_dev, pixels, chans)
    return (mixed, latent_grad, temporal_grad)


def solution(mesh):
    placed = (
        P("dp", "frames", None, None),
        P("dp", "frames", None),
        P("dp"),
        P(),
        P(),
        P(),
        P(),
        P("dp", None),
        P("dp", None),
        P("dp", "frames", None, None),
    )
    return jax.shard_map(
        per_device,
        mesh=mesh,
        in_specs=placed,
        out_specs=(P("dp", "frames", None, None), P("dp", "frames", None, None), P("dp", None)),
        check_vma=False,
    )
```

profile of v0, /device:TPU:2, one launch (start us, length us, event | category | flops | bytes accessed | tf_op | source)
XLA Modules:
  0.0 397.9 jit_solution(13264229665452093458)
XLA Ops:
  8.7 2.0 copy.100
  10.7 6.2 %all-to-all-start.2 = ((bf16[1,2,144,640]{3,1,0,2:T(2,128)(2,1)}), bf16[1,2,144,640]{3,1,0,2:T(2,128)(2,1)S(1)}, u32[]{:S(2)}, u32[]{:S(2)}) async-start(bf16[1,2,144,640]{3,1,0,2:T(2,128)(2,1)} %copy.100), calls=%async_computation.2 | async-start | bytes 737280 | tf_op jit(solution)/shard_map/all_to_all | solution.py:108
  26.3 59.8 %all-gather.5.cloned.1.call-done = bf16[32,180,640]{2,1,0:T(8,128)(2,1)} async-done(((bf16[1,180,640]{2,1,0:T(8,128)(2,1)}), bf16[32,180,640]{2,1,0:T(8,128)(2,1)}) %all-gather.5.cloned.1.call-update) | async-done | bytes 7372816 | tf_op jit(solution)/shard_map/all_gather | solution.py:89
  86.1 8.8 %reshape.259 = bf16[5760,640,1]{1,0,2:T(8,128)(2,1)} reshape(bf16[32,180,640]{2,1,0:T(8,128)(2,1)} %all-gather.5.cloned.1.call-done) | data formatting | bytes 14745600
  94.9 7.0 %fusion.50 = bf16[1,2,144,640]{3,2,1,0:T(8,128)(2,1)S(1)} fusion(bf16[2,144,5760]{2,1,0:T(8,128)(2,1)} %copy-done.11, bf16[5760,640,1]{1,0,2:T(8,128)(2,1)} %reshape.259, f32[640]{0:T(1024)S(1)} %convolution_reduce_fusion), kind=kOutput, calls=%fused_computation.24 | convolution fusion | flops 2123735040 | bytes 11061760 | tf_op jit(solution)/shard_map/dot_general | solution.py:87
  102.9 7.0 %all-to-all-start = ((bf16[1,2,144,640]{3,1,0,2:T(2,128)(2,1)}), bf16[1,2,144,640]{3,1,0,2:T(2,128)(2,1)S(1)}, u32[]{:S(2)}, u32[]{:S(2)}) async-start(bf16[1,2,144,640]{3,1,0,2:T(2,128)(2,1)} %copy.92), calls=%async_computation | async-start | bytes 737280 | tf_op jit(solution)/shard_map/all_to_all | solution.py:96
  114.9 30.0 %all-gather.7.cloned.1.call-done = bf16[32,60,640]{2,1,0:T(8,128)(2,1)} async-done(((bf16[1,60,640]{2,1,0:T(8,128)(2,1)}), bf16[32,60,640]{2,1,0:T(8,128)(2,1)}) %all-gather.7.cloned.1.call-update) | async-done | bytes 2457616 | tf_op jit(solution)/shard_map/all_gather | solution.py:103
  144.9 4.1 %reshape.262 = bf16[1920,640,1]{1,0,2:T(8,128)(2,1)} reshape(bf16[32,60,640]{2,1,0:T(8,128)(2,1)} %all-gather.7.cloned.1.call-done) | data formatting | bytes 4915200
  149.0 4.1 %reshape.263 = bf16[3,640,640,1]{2,1,0,3:T(8,128)(2,1)} reshape(bf16[32,60,640]{2,1,0:T(8,128)(2,1)} %all-gather.7.cloned.1.call-done) | data formatting | bytes 4915200 | tf_op jit(solution)/shard_map/reshape | solution.py:115
  153.1 8.8 %reshape.265 = bf16[9,640,640,1]{2,1,0,3:T(8,128)(2,1)} reshape(bf16[32,180,640]{2,1,0:T(8,128)(2,1)} %all-gather.5.cloned.1.call-done) | data formatting | bytes 14745600 | tf_op jit(solution)/shard_map/reshape | solution.py:139
  166.3 3.8 fusion.76
  170.1 98.5 %fusion = f32[64,640]{1,0:T(8,128)S(1)} fusion(f32[1920,640]{1,0:T(8,128)} %fusion.76), kind=kCustom, calls=%all-reduce-scatter | all-reduce-scatter fusion | flops 1310721 | bytes 5080064
  268.6 2.2 collective-permute-start
  271.3 2.0 collective-permute-start.1
  273.3 3.6 fusion.45
  276.9 4.1 %all-to-all-start.3 = ((bf16[1,16,18,640]{3,2,0,1:T(8,128)(2,1)}), bf16[1,16,18,640]{3,2,0,1:T(8,128)(2,1)}, u32[]{:S(2)}, u32[]{:S(2)}) async-start(bf16[1,16,18,640]{3,2,0,1:T(8,128)(2,1)} %fusion.45), calls=%async_computation.3 | async-start | bytes 983040 | tf_op jit(solution)/shard_map/all_to_all | solution.py:133
  281.1 4.7 %concatenate.49 = f32[188,640]{1,0:T(8,128)} concatenate(f32[60,640]{1,0:T(8,128)} %collective-permute-done.1, f32[64,640]{1,0:T(8,128)} %collective-permute-done, f32[64,640]{1,0:T(8,128)S(1)} %fusion), dimensions={0} | concatenate | bytes 962560
  287.4 3.1 fusion.26
  292.2 66.7 %all-reduce.8.cloned.1.call-done = f32[60,640]{1,0:T(8,128)} async-done(((f32[60,640]{1,0:T(8,128)}), f32[60,640]{1,0:T(8,128)}) %all-reduce.8.cloned.1.call-update) | async-done | bytes 153616 | tf_op jit(solution)/shard_map/psum | solution.py:132
  360.4 4.6 %all-to-all-start.1 = ((f32[1,16,18,640]{3,0,2,1:T(1,128)}), f32[1,16,18,640]{3,0,2,1:T(1,128)S(1)}, u32[]{:S(2)}, u32[]{:S(2)}) async-start(f32[1,16,18,640]{3,0,2,1:T(1,128)} %copy.98), calls=%async_computation.1 | async-start | bytes 1474560 | tf_op jit(solution)/shard_map/all_to_all | solution.py:107
  369.6 2.0 copy.111
  371.6 7.2 %reshape_reshape.7 = bf16[288,9,640]{2,1,0:T(8,128)(2,1)} reshape(bf16[2,9,16,5760]{3,2,1,0:T(8,128)(2,1)} %copy.111) | data formatting | bytes 6635520 | tf_op jit(solution)/shard_map/reshape;reshape | solution.py:138
  378.8 3.4 copy.112
  382.2 6.1 %fusion.60 = (f32[2,640]{1,0:T(2,128)S(1)}, f32[2,144,640]{2,1,0:T(8,128)S(1)}) fusion(f32[1,2,144,640]{3,2,1,0:T(8,128)S(1)} %get-tuple-element.42, f32[2,640]{1,0:T(2,128)S(1)} %mul.161, f32[2,640]{1,0:T(2,128)S(1)} %sub.66, f32[640]{0:T(1024)S(1)} %copy-done.12, f32[640]{0:T(1024)S(1)} %copy-done.13, bf16[2,144,640,9]{2,1,0,3:T(8,128)(2,1)S(1)} %bitcast.165, ...), kind=kOutput, calls=%fused_computation.47 | convolution fusion | flops 2126498560 | bytes 12185600 | tf_op jit(solution)/shard_map/rtc,tkc->rk/dot_general | solution.py:136
  (111 shorter events, 32.7 us)
Async XLA Ops:
  7.2 18.6 %copy-start = (f32[320,640]{1,0:T(8,128)S(1)}, f32[320,640]{1,0:T(8,128)}, u32[]{:S(2)}) copy-start(f32[320,640]{1,0:T(8,128)} %param.16) | copy-start | bytes 2457604
  7.2 78.9 %all-gather.5.cloned.1.call-start = ((), (), s32[]{:S(2)}) async-start(), calls=%async_computation.5 | async-start | bytes 7772160 | tf_op jit(solution)/shard_map/all_gather | solution.py:89
  7.9 137.0 %all-gather.7.cloned.1.call-start = ((), (), s32[]{:S(2)}) async-start(), calls=%async_computation.6 | async-start | bytes 2703360 | tf_op jit(solution)/shard_map/all_gather | solution.py:103
  10.7 92.2 %all-to-all-start.2 = ((bf16[1,2,144,640]{3,1,0,2:T(2,128)(2,1)}), bf16[1,2,144,640]{3,1,0,2:T(2,128)(2,1)S(1)}, u32[]{:S(2)}, u32[]{:S(2)}) async-start(bf16[1,2,144,640]{3,1,0,2:T(2,128)(2,1)} %copy.100), calls=%async_computation.2 | async-start | bytes 737280 | tf_op jit(solution)/shard_map/all_to_all | solution.py:108
  22.8 0.7 copy-start.12
  22.8 0.7 copy-start.13
  24.0 1.7 copy-start.11
  102.9 59.0 %all-to-all-start = ((bf16[1,2,144,640]{3,1,0,2:T(2,128)(2,1)}), bf16[1,2,144,640]{3,1,0,2:T(2,128)(2,1)S(1)}, u32[]{:S(2)}, u32[]{:S(2)}) async-start(bf16[1,2,144,640]{3,1,0,2:T(2,128)(2,1)} %copy.92), calls=%async_computation | async-start | bytes 737280 | tf_op jit(solution)/shard_map/all_to_all | solution.py:96
  162.4 0.8 copy-start.3
  162.5 0.9 copy-start.5
  162.5 1.1 copy-start.7
  162.5 3.9 copy-start.10
  268.6 4.7 %copy-start.2 = (bf16[3,640,640,1]{2,1,0,3:T(8,128)(2,1)S(1)}, bf16[3,640,640,1]{2,1,0,3:T(8,128)(2,1)}, u32[]{:S(2)}) copy-start(bf16[3,640,640,1]{2,1,0,3:T(8,128)(2,1)} %reshape.263) | copy-start | bytes 7372804
  268.6 4.7 %copy-start.9 = (bf16[288,3,640]{2,1,0:T(4,128)(2,1)S(1)}, bf16[288,3,640]{2,1,0:T(4,128)(2,1)}, u32[]{:S(2)}) copy-start(bf16[288,3,640]{2,1,0:T(4,128)(2,1)} %reshape_reshape.6) | copy-start | bytes 3317764
  268.6 12.4 %collective-permute-start = (f32[64,640]{1,0:T(8,128)S(1)}, f32[64,640]{1,0:T(8,128)}, u32[]{:S(2)}, u32[]{:S(2)}) collective-permute-start(f32[64,640]{1,0:T(8,128)S(1)} %fusion), channel_id=1, source_target_pairs={{0,1},{1,2},{2,3},{3,4},{4,5},{5,6},{6,7},{7,8},{8,9},{9,10},{10,1... | collective-permute-start | bytes 491528
  271.3 9.7 %collective-permute-start.1 = (f32[60,640]{1,0:T(8,128)S(1)}, f32[60,640]{1,0:T(8,128)}, u32[]{:S(2)}, u32[]{:S(2)}) collective-permute-start(f32[60,640]{1,0:T(8,128)S(1)} %slice.90), channel_id=1, source_target_pairs={{0,2},{1,3},{2,4},{3,5},{4,6},{5,7},{6,8},{7,9},{8,10},{9,11},{10,... | collective-permute-start | bytes 460808
  273.3 14.1 %copy-start.4 = (bf16[1,16,18,640]{3,2,1,0:T(8,128)(2,1)S(1)}, bf16[1,16,18,640]{3,2,1,0:T(8,128)(2,1)}, u32[]{:S(2)}) copy-start(bf16[1,16,18,640]{3,2,1,0:T(8,128)(2,1)} %copy-done.3) | copy-start | bytes 1105924
  273.3 14.1 %copy-start.6 = (bf16[1,16,18,640]{3,2,1,0:T(8,128)(2,1)S(1)}, bf16[1,16,18,640]{3,2,1,0:T(8,128)(2,1)}, u32[]{:S(2)}) copy-start(bf16[1,16,18,640]{3,2,1,0:T(8,128)(2,1)} %copy-done.5) | copy-start | bytes 1105924
  273.3 14.1 %copy-start.8 = (bf16[1,16,18,640]{3,2,1,0:T(8,128)(2,1)S(1)}, bf16[1,16,18,640]{3,2,1,0:T(8,128)(2,1)}, u32[]{:S(2)}) copy-start(bf16[1,16,18,640]{3,2,1,0:T(8,128)(2,1)} %copy-done.7) | copy-start | bytes 1105924
  276.9 83.5 %all-to-all-start.3 = ((bf16[1,16,18,640]{3,2,0,1:T(8,128)(2,1)}), bf16[1,16,18,640]{3,2,0,1:T(8,128)(2,1)}, u32[]{:S(2)}, u32[]{:S(2)}) async-start(bf16[1,16,18,640]{3,2,0,1:T(8,128)(2,1)} %fusion.45), calls=%async_computation.3 | async-start | bytes 983040 | tf_op jit(solution)/shard_map/all_to_all | solution.py:133
  281.0 77.8 %all-reduce.8.cloned.1.call-start = ((), (), s32[]{:S(2)}) async-start(), calls=%async_computation.4 | async-start | bytes 327680 | tf_op jit(solution)/shard_map/psum | solution.py:132
  360.4 29.6 %all-to-all-start.1 = ((f32[1,16,18,640]{3,0,2,1:T(1,128)}), f32[1,16,18,640]{3,0,2,1:T(1,128)S(1)}, u32[]{:S(2)}, u32[]{:S(2)}) async-start(f32[1,16,18,640]{3,0,2,1:T(1,128)} %copy.98), calls=%async_computation.1 | async-start | bytes 1474560 | tf_op jit(solution)/shard_map/all_to_all | solution.py:107
  382.2 9.2 %copy-start.1 = (f32[320,640]{1,0:T(8,128)S(1)}, f32[320,640]{1,0:T(8,128)}, u32[]{:S(2)}) copy-start(f32[320,640]{1,0:T(8,128)} %param.16) | copy-start | bytes 2457604
Sparse Core Ops, SparseCore 0:
  10.6 75.4 all-gather.4
  88.6 56.2 all-gather.6
  287.5 71.3 all-reduce.7
where the time goes:
time: 400 us; the launch traced here: 398 us
  waiting for transfers between devices  158 us (40%)
  blocking collectives  98.5 us (25%)
  local copies, waits for them, and re-layouts  67.7 us (17%)
  starting transfers between devices  26.2 us (7%)
  matrix products  25.7 us (6%)
  between operations  15.6 us (4%)
  other arithmetic  6.41 us (2%)
    unnamed x1, blocking collectives  98.5 us
    psum x1, waiting for transfers between devices, per_device(): temporal_grad = lax.psum(owned, 'frames') * factor  66.7 us
    all_gather x1, waiting for transfers between devices, per_device(): lax.all_gather(spatial_weight, 'dp', axis=0, tiled=True)  59.8 us
    all_gather x1, waiting for transfers between devices, per_device(): lax.all_gather(temporal_weight, 'dp', axis=0, tiled=True)  30 us
    unnamed x51, local copies, waits for them, and re-layouts  29.5 us
    reshape x1, local copies, waits for them, and re-layouts, per_device(): spatial_back.reshape(9, chans, chans)  8.79 us
  transfers between devices with their start and end apart: 9, of which 3 were waited for; matrix products, arithmetic and copies ran while one was open for 22% of the time, Pallas kernels for 0%

commit v1 on v0

--- a/solution.py
+++ b/solution.py
@@ -100,7 +100,9 @@
     columns = moved_cols
     temporal_out = jnp.dot(
         columns,
-        lax.all_gather(temporal_weight, "dp", axis=0, tiled=True),
+        jnp.concatenate(
+            lax.all_to_all(jnp.stack([temporal_weight] * lax.axis_size("dp")), "dp", 0, 0), axis=0
+        ),
         preferred_element_type=jnp.float32,
     )
     local_mixed = local_out.astype(jnp.float32) + temporal_out.reshape(local_out.shape)

time: 400 us -> 437 us (1.093)
  waiting for transfers between devices: 158 us -> 174 us
  blocking collectives: 98.5 us -> 111 us
  starting transfers between devices: 26.2 us -> 35.2 us
    all_gather x1, waiting for transfers between devices: 59.8 us -> 80.5 us  [per_device(): lax.all_gather(spatial_weight, 'dp', axis=0, tiled=True)]
    all_to_all x0 -> x1, blocking collectives: none -> 12.9 us  [per_device(): lax.all_to_all(cotangent, 'frames', split_axis=2, concat_axis=1, tiled=True)]
    unnamed x51 -> x58, local copies, waits for them, and re-layouts: 29.5 us -> 23.7 us
    all_gather x1, waiting for transfers between devices: 30 us -> 25.2 us  [per_device(): temporal_back = lax.all_gather(temporal_weight, 'dp', axis=0, tiled=True)]
    all_to_all x1, starting transfers between devices: 6.18 us -> 10.8 us  [per_device(): lax.all_to_all(jnp.stack([temporal_weight] * lax.axis_size('dp')), 'dp',...]
  transfers between devices with their start and end apart: 9 -> 9, of which waited for: 3 -> 3; matrix products, arithmetic and copies ran while one was open for 22% -> 20% of each run, Pallas kernels for 0% -> 0%
where the time goes in v1:
time: 437 us; the launch traced here: 435 us
  waiting for transfers between devices  174 us (40%)
  blocking collectives  111 us (25%)
  local copies, waits for them, and re-layouts  68.8 us (16%)
  starting transfers between devices  35.2 us (8%)
  matrix products  24.6 us (6%)
  between operations  15.6 us (4%)
  other arithmetic  5.72 us (1%)
    unnamed x1, blocking collectives  98.3 us
    all_gather x1, waiting for transfers between devices, per_device(): lax.all_gather(spatial_weight, 'dp', axis=0, tiled=True)  80.5 us
    psum x1, waiting for transfers between devices, per_device(): temporal_grad = lax.psum(owned, 'frames') * factor  66.7 us
    all_gather x1, waiting for transfers between devices, per_device(): temporal_back = lax.all_gather(temporal_weight, 'dp', axis=0, tiled=True)  25.2 us
    unnamed x58, local copies, waits for them, and re-layouts  23.7 us
    all_to_all x1, blocking collectives, per_device(): lax.all_to_all(cotangent, 'frames', split_axis=2, concat_axis=1, tiled=True)  12.9 us
    all_to_all x1, starting transfers between devices, per_device(): lax.all_to_all(spatial_out, 'frames', split_axis=2, concat_axis=1, tiled=...  11.3 us
    all_to_all x1, starting transfers between devices, per_device(): lax.all_to_all(jnp.stack([temporal_weight] * lax.axis_size('dp')), 'dp',...  10.8 us
  transfers between devices with their start and end apart: 9, of which 3 were waited for; matrix products, arithmetic and copies ran while one was open for 20% of the time, Pallas kernels for 0%

profile of v1, /device:TPU:2, one launch (start us, length us, event | category | flops | bytes accessed | tf_op | source)
XLA Modules:
  0.0 435.0 jit_solution(15747827357753693809)
XLA Ops:
  9.2 12.9 %all_to_all.74 = bf16[1,2,144,640]{3,1,0,2:T(2,128)(2,1)S(1)} all-to-all(bf16[1,2,144,640]{3,1,0,2:T(2,128)(2,1)S(1)} %copy.100), channel_id=1, replica_groups=mesh['frames'=8,'dp'=32] {'frames'}, dimensions={2} | all-to-all | bytes 737280 | tf_op jit(solution)/shard_map/all_to_all | solution.py:110
  22.1 2.8 stack.2
  25.0 10.8 %all-to-all-start.1 = ((bf16[32,60,640]{2,1,0:T(8,128)(2,1)}), bf16[32,60,640]{2,1,0:T(8,128)(2,1)}, u32[]{:S(2)}, u32[]{:S(2)}) async-start(bf16[32,60,640]{2,1,0:T(8,128)(2,1)} %stack.2), calls=%async_computation.1 | async-start | bytes 5242880 | tf_op jit(solution)/shard_map/all_to_all | solution.py:104
  43.4 80.5 %all-gather.5.cloned.1.call-done = bf16[32,180,640]{2,1,0:T(8,128)(2,1)} async-done(((bf16[1,180,640]{2,1,0:T(8,128)(2,1)}), bf16[32,180,640]{2,1,0:T(8,128)(2,1)}) %all-gather.5.cloned.1.call-update) | async-done | bytes 7372816 | tf_op jit(solution)/shard_map/all_gather | solution.py:89
  123.9 8.8 %reshape.265 = bf16[5760,640,1]{1,0,2:T(8,128)(2,1)} reshape(bf16[32,180,640]{2,1,0:T(8,128)(2,1)} %all-gather.5.cloned.1.call-done) | data formatting | bytes 14745600
  132.7 6.9 %fusion.50 = bf16[1,2,144,640]{3,2,1,0:T(8,128)(2,1)S(1)} fusion(bf16[2,144,5760]{2,1,0:T(8,128)(2,1)} %copy-done.13, bf16[5760,640,1]{1,0,2:T(8,128)(2,1)} %reshape.265, f32[640]{0:T(1024)S(1)} %convolution_reduce_fusion), kind=kOutput, calls=%fused_computation.24 | convolution fusion | flops 2123735040 | bytes 11061760 | tf_op jit(solution)/shard_map/dot_general | solution.py:87
  140.6 11.3 %all-to-all-start = ((bf16[1,2,144,640]{3,1,0,2:T(2,128)(2,1)}), bf16[1,2,144,640]{3,1,0,2:T(2,128)(2,1)S(1)}, u32[]{:S(2)}, u32[]{:S(2)}) async-start(bf16[1,2,144,640]{3,1,0,2:T(2,128)(2,1)} %copy.92), calls=%async_computation | async-start | bytes 737280 | tf_op jit(solution)/shard_map/all_to_all | solution.py:96
  157.0 4.1 reshape.268
  161.1 25.2 %all-gather.7.cloned.1.call-done = bf16[32,60,640]{2,1,0:T(8,128)(2,1)} async-done(((bf16[1,60,640]{2,1,0:T(8,128)(2,1)}), bf16[32,60,640]{2,1,0:T(8,128)(2,1)}) %all-gather.7.cloned.1.call-update) | async-done | bytes 2457616 | tf_op jit(solution)/shard_map/all_gather | solution.py:113
  186.3 4.1 reshape.269
  190.5 8.8 %reshape.271 = bf16[9,640,640,1]{2,1,0,3:T(8,128)(2,1)} reshape(bf16[32,180,640]{2,1,0:T(8,128)(2,1)} %all-gather.5.cloned.1.call-done) | data formatting | bytes 14745600 | tf_op jit(solution)/shard_map/reshape | solution.py:141
  203.7 3.8 fusion.76
  207.5 98.3 %fusion = f32[64,640]{1,0:T(8,128)S(1)} fusion(f32[1920,640]{1,0:T(8,128)} %fusion.76), kind=kCustom, calls=%all-reduce-scatter | all-reduce-scatter fusion | flops 1310721 | bytes 5080064
  305.8 2.2 collective-permute-start
  310.5 3.6 fusion.45
  314.1 4.1 all-to-all-start.4
  318.3 4.6 %concatenate.49 = f32[188,640]{1,0:T(8,128)} concatenate(f32[60,640]{1,0:T(8,128)} %collective-permute-done.1, f32[64,640]{1,0:T(8,128)} %collective-permute-done, f32[64,640]{1,0:T(8,128)S(1)} %fusion), dimensions={0} | concatenate | bytes 962560
  324.6 3.1 fusion.26
  329.4 66.7 %all-reduce.8.cloned.1.call-done = f32[60,640]{1,0:T(8,128)} async-done(((f32[60,640]{1,0:T(8,128)}), f32[60,640]{1,0:T(8,128)}) %all-reduce.8.cloned.1.call-update) | async-done | bytes 153616 | tf_op jit(solution)/shard_map/psum | solution.py:134
  397.6 4.6 %all-to-all-start.2 = ((f32[1,16,18,640]{3,0,2,1:T(1,128)}), f32[1,16,18,640]{3,0,2,1:T(1,128)S(1)}, u32[]{:S(2)}, u32[]{:S(2)}) async-start(f32[1,16,18,640]{3,0,2,1:T(1,128)} %copy.98), calls=%async_computation.2 | async-start | bytes 1474560 | tf_op jit(solution)/shard_map/all_to_all | solution.py:109
  406.7 2.0 copy.111
  408.8 7.1 %reshape_reshape.7 = bf16[288,9,640]{2,1,0:T(8,128)(2,1)} reshape(bf16[2,9,16,5760]{3,2,1,0:T(8,128)(2,1)} %copy.111) | data formatting | bytes 6635520 | tf_op jit(solution)/shard_map/reshape;reshape | solution.py:140
  415.9 3.4 copy.112
  419.3 6.1 %fusion.60 = (f32[2,640]{1,0:T(2,128)S(1)}, f32[2,144,640]{2,1,0:T(8,128)S(1)}) fusion(f32[1,2,144,640]{3,2,1,0:T(8,128)S(1)} %get-tuple-element.42, f32[2,640]{1,0:T(2,128)S(1)} %mul.161, f32[2,640]{1,0:T(2,128)S(1)} %sub.66, f32[640]{0:T(1024)S(1)} %copy-done.14, f32[640]{0:T(1024)S(1)} %copy-done.15, bf16[2,144,640,9]{2,1,0,3:T(8,128)(2,1)S(1)} %bitcast.165, ...), kind=kOutput, calls=%fused_computation.47 | convolution fusion | flops 2126498560 | bytes 12185600 | tf_op jit(solution)/shard_map/rtc,tkc->rk/dot_general | solution.py:138
  (121 shorter events, 33.3 us)
Async XLA Ops:
  7.2 35.7 %copy-start = (f32[320,640]{1,0:T(8,128)S(1)}, f32[320,640]{1,0:T(8,128)}, u32[]{:S(2)}) copy-start(f32[320,640]{1,0:T(8,128)} %param.16) | copy-start | bytes 2457604
  7.2 116.7 %all-gather.5.cloned.1.call-start = ((), (), s32[]{:S(2)}) async-start(), calls=%async_computation.6 | async-start | bytes 7772160 | tf_op jit(solution)/shard_map/all_gather | solution.py:89
  24.9 11.6 %copy-start.11 = (bf16[1,2,144,640]{3,2,1,0:T(8,128)(2,1)S(1)}, bf16[1,2,144,640]{3,2,1,0:T(8,128)(2,1)}, u32[]{:S(2)}) copy-start(bf16[1,2,144,640]{3,2,1,0:T(8,128)(2,1)} %param.10) | copy-start | bytes 1105924
  24.9 11.7 %copy-start.12 = (f32[19,640]{1,0:T(8,128)S(1)}, f32[19,640]{1,0:T(8,128)}, u32[]{:S(2)}) copy-start(f32[19,640]{1,0:T(8,128)} %param.15) | copy-start | bytes 145924
  24.9 11.7 %copy-start.16 = (s32[1,2,144]{2,1,0:T(2,128)S(1)}, s32[1,2,144]{2,1,0:T(2,128)}, u32[]{:S(2)}) copy-start(s32[1,2,144]{2,1,0:T(2,128)} %param.11) | copy-start | bytes 3460
  24.9 13.7 %copy-start.17 = (u32[256]{0:T(256)S(1)}, u32[256]{0:T(256)}, u32[]{:S(2)}) copy-start(u32[256]{0:T(256)} %constant.44) | copy-start | bytes 3076
  24.9 15.0 %copy-start.14 = (f32[640]{0:T(1024)S(1)}, f32[640]{0:T(1024)}, u32[]{:S(2)}) copy-start(f32[640]{0:T(1024)} %param.14) | copy-start | bytes 7684
  24.9 15.0 %copy-start.15 = (f32[640]{0:T(1024)S(1)}, f32[640]{0:T(1024)}, u32[]{:S(2)}) copy-start(f32[640]{0:T(1024)} %param.13) | copy-start | bytes 7684
  25.0 115.7 %all-to-all-start.1 = ((bf16[32,60,640]{2,1,0:T(8,128)(2,1)}), bf16[32,60,640]{2,1,0:T(8,128)(2,1)}, u32[]{:S(2)}, u32[]{:S(2)}) async-start(bf16[32,60,640]{2,1,0:T(8,128)(2,1)} %stack.2), calls=%async_computation.1 | async-start | bytes 5242880 | tf_op jit(solution)/shard_map/all_to_all | solution.py:104
  35.8 150.5 %all-gather.7.cloned.1.call-start = ((), (), s32[]{:S(2)}) async-start(), calls=%async_computation.7 | async-start | bytes 2703360 | tf_op jit(solution)/shard_map/all_gather | solution.py:113
  41.2 1.7 copy-start.13
  140.6 58.6 %all-to-all-start = ((bf16[1,2,144,640]{3,1,0,2:T(2,128)(2,1)}), bf16[1,2,144,640]{3,1,0,2:T(2,128)(2,1)S(1)}, u32[]{:S(2)}, u32[]{:S(2)}) async-start(bf16[1,2,144,640]{3,1,0,2:T(2,128)(2,1)} %copy.92), calls=%async_computation | async-start | bytes 737280 | tf_op jit(solution)/shard_map/all_to_all | solution.py:96
  199.8 3.9 copy-start.10
  305.8 4.7 %copy-start.2 = (bf16[3,640,640,1]{2,1,0,3:T(8,128)(2,1)S(1)}, bf16[3,640,640,1]{2,1,0,3:T(8,128)(2,1)}, u32[]{:S(2)}) copy-start(bf16[3,640,640,1]{2,1,0,3:T(8,128)(2,1)} %reshape.269) | copy-start | bytes 7372804
  305.8 4.7 %copy-start.9 = (bf16[288,3,640]{2,1,0:T(4,128)(2,1)S(1)}, bf16[288,3,640]{2,1,0:T(4,128)(2,1)}, u32[]{:S(2)}) copy-start(bf16[288,3,640]{2,1,0:T(4,128)(2,1)} %reshape_reshape.6) | copy-start | bytes 3317764
  305.8 12.5 %collective-permute-start = (f32[64,640]{1,0:T(8,128)S(1)}, f32[64,640]{1,0:T(8,128)}, u32[]{:S(2)}, u32[]{:S(2)}) collective-permute-start(f32[64,640]{1,0:T(8,128)S(1)} %fusion), channel_id=1, source_target_pairs={{0,1},{1,2},{2,3},{3,4},{4,5},{5,6},{6,7},{7,8},{8,9},{9,10},{10,1... | collective-permute-start | bytes 491528
  308.5 9.8 %collective-permute-start.1 = (f32[60,640]{1,0:T(8,128)S(1)}, f32[60,640]{1,0:T(8,128)}, u32[]{:S(2)}, u32[]{:S(2)}) collective-permute-start(f32[60,640]{1,0:T(8,128)S(1)} %slice.90), channel_id=1, source_target_pairs={{0,2},{1,3},{2,4},{3,5},{4,6},{5,7},{6,8},{7,9},{8,10},{9,11},{10,... | collective-permute-start | bytes 460808
  310.5 14.1 %copy-start.4 = (bf16[1,16,18,640]{3,2,1,0:T(8,128)(2,1)S(1)}, bf16[1,16,18,640]{3,2,1,0:T(8,128)(2,1)}, u32[]{:S(2)}) copy-start(bf16[1,16,18,640]{3,2,1,0:T(8,128)(2,1)} %copy-done.3) | copy-start | bytes 1105924
  310.5 14.1 %copy-start.6 = (bf16[1,16,18,640]{3,2,1,0:T(8,128)(2,1)S(1)}, bf16[1,16,18,640]{3,2,1,0:T(8,128)(2,1)}, u32[]{:S(2)}) copy-start(bf16[1,16,18,640]{3,2,1,0:T(8,128)(2,1)} %copy-done.5) | copy-start | bytes 1105924
  310.5 14.1 %copy-start.8 = (bf16[1,16,18,640]{3,2,1,0:T(8,128)(2,1)S(1)}, bf16[1,16,18,640]{3,2,1,0:T(8,128)(2,1)}, u32[]{:S(2)}) copy-start(bf16[1,16,18,640]{3,2,1,0:T(8,128)(2,1)} %copy-done.7) | copy-start | bytes 1105924
  314.1 83.5 %all-to-all-start.4 = ((bf16[1,16,18,640]{3,2,0,1:T(8,128)(2,1)}), bf16[1,16,18,640]{3,2,0,1:T(8,128)(2,1)}, u32[]{:S(2)}, u32[]{:S(2)}) async-start(bf16[1,16,18,640]{3,2,0,1:T(8,128)(2,1)} %fusion.45), calls=%async_computation.4 | async-start | bytes 983040 | tf_op jit(solution)/shard_map/all_to_all | solution.py:135
  318.2 77.8 %all-reduce.8.cloned.1.call-start = ((), (), s32[]{:S(2)}) async-start(), calls=%async_computation.5 | async-start | bytes 327680 | tf_op jit(solution)/shard_map/psum | solution.py:134
  397.6 29.5 %all-to-all-start.2 = ((f32[1,16,18,640]{3,0,2,1:T(1,128)}), f32[1,16,18,640]{3,0,2,1:T(1,128)S(1)}, u32[]{:S(2)}, u32[]{:S(2)}) async-start(f32[1,16,18,640]{3,0,2,1:T(1,128)} %copy.98), calls=%async_computation.2 | async-start | bytes 1474560 | tf_op jit(solution)/shard_map/all_to_all | solution.py:109
  419.3 9.2 %copy-start.1 = (f32[320,640]{1,0:T(8,128)S(1)}, f32[320,640]{1,0:T(8,128)}, u32[]{:S(2)}) copy-start(f32[320,640]{1,0:T(8,128)} %param.16) | copy-start | bytes 2457604
  (3 other events, 2.8 us)
Sparse Core Ops, SparseCore 0:
  10.6 113.3 all-gather.4
  126.5 59.8 all-gather.6
  324.7 71.2 all-reduce.7
